TPU v7x, 32 devices: a whole 2x2x4 slice. The times are simulated.
32 devices in a mesh: dict: 4 (over z), scan: 8 (over y, x, core).
Axes of the slice: x: 2, y: 2, z: 4, core: 2. Of those that a mesh axis runs over, the one named last changes fastest.
Arguments:
- patterns: float32 [128, 64, 3600], P('scan', 'dict'), may hold values from -63 to 63
- background: float32 [3600], replicated, may hold values from -6 to 6
- templates: bfloat16 [512, 3600], P('dict'), may hold values from -19.5 to 19.5
- grain_id: int32 [128, 64], P('scan', 'dict'), may hold values from 0 to 31
- keep_mask: int32 [128, 64], P('scan', 'dict'), may hold values 0 or 1
- grain_row: int32 [32], replicated, may hold values from 0 to 31, each once
Outputs:
- max_score: float32 [128, 64], P('scan', 'dict')
- grain_patterns: float32 [32, 3600], P('scan')
Inputs may be any that keep to these rules, and one draw needn't show every extreme that they name: grain_row holds each of 0 to 31 once.
All inputs are finite; a program needn't handle non-finite values. No bound on the sum of `keep_mask` on one device may be relied on, other than what follows from the above.
Results may differ from a plain program's by a relative error of at most 0.0045.
Values may be sent and summed in bfloat16 or wider, within the bound.
A program may use at most 128 MiB of HBM per device.

v0:
```python
import math

import jax
import jax.numpy as jnp
from jax import lax
from jax.sharding import PartitionSpec as P


def with_halo(block, sides, width):
    for axis, dim in sides:
        count = lax.axis_size(axis)
        forward = [(i, i + 1) for i in range(count - 1)]
        backward = [(target, source) for source, target in forward]
        low = lax.ppermute(
            lax.slice_in_dim(block, block.shape[dim] - width, None, axis=dim), axis, forward
        )
        high = lax.ppermute(lax.slice_in_dim(block, 0, width, axis=dim), axis, backward)
        block = jnp.concatenate([low, block, high], axis=dim)
    return block


def unit_rows(values):
    mean_square = jnp.mean(values * values, axis=-1, keepdims=True)
    return values * lax.rsqrt(mean_square + 1e-05)


def filter_points(measured, background):
    centered = measured - background
    centered = centered - jnp.mean(centered, axis=-1, keepdims=True)
    return unit_rows(centered).astype(jnp.bfloat16)


def shards(patterns, background, templates, grain_id, keep_mask, grain_row):
    tile_rows, tile_cols, pixels = patterns.shape
    filtered = filter_points(patterns, background)
    padded = with_halo(filtered, (("dict", 1), ("scan", 0)), 1)
    neighbour = jnp.zeros((tile_rows, tile_cols, pixels), jnp.float32)
    for row_shift in range(3):
        for col_shift in range(3):
            neighbour = neighbour + padded[
                row_shift : row_shift + tile_rows, col_shift : col_shift + tile_cols
            ].astype(jnp.float32)
    indexed = unit_rows(neighbour).astype(jnp.bfloat16).reshape(tile_rows * tile_cols, pixels)
    point_count = indexed.shape[0]
    centered_panel = templates.astype(jnp.float32)
    centered_panel = centered_panel - jnp.mean(centered_panel, axis=-1, keepdims=True)
    unit_panel = unit_rows(centered_panel).astype(jnp.bfloat16)
    lowest = jnp.full((point_count,), -1e30, jnp.float32)
    scores = lax.dot_general(
        indexed,
        lax.all_gather(unit_panel, "dict", axis=0, tiled=True),
        (((1,), (1,)), ((), ())),
        preferred_element_type=jnp.float32,
    )
    best_dot = jnp.maximum(lowest, jnp.max(scores, axis=1))
    root_inverse = 1.0 / math.sqrt(pixels)
    max_score = (best_dot * root_inverse).reshape(tile_rows, tile_cols)
    point_grain = grain_id.reshape(-1)
    point_keep = keep_mask.reshape(-1)
    grain_count = grain_row.shape[0]
    grain_index = jnp.arange(grain_count, dtype=jnp.int32)
    matches = point_grain[:, None] == grain_index[None, :]
    point_row = jnp.sum(jnp.where(matches, grain_row[None, :], 0), axis=1)
    selector = ((point_row[:, None] == grain_index[None, :]) & (point_keep[:, None] == 1)).astype(
        jnp.bfloat16
    )
    partial_rows = lax.psum_scatter(
        lax.dot_general(
            selector, indexed, (((0,), (0,)), ((), ())), preferred_element_type=jnp.float32
        ).astype(jnp.bfloat16),
        "scan",
        scatter_dimension=0,
        tiled=True,
    ).astype(jnp.float32)
    grain_total = lax.psum(partial_rows, "dict")
    grain_patterns = unit_rows(grain_total)
    return (max_score, grain_patterns)


def solution(mesh):
    return jax.shard_map(
        shards,
        mesh=mesh,
        in_specs=(
            P("scan", "dict", None),
            P(),
            P("dict", None),
            P("scan", "dict"),
            P("scan", "dict"),
            P(),
        ),
        out_specs=(P("scan", "dict"), P("scan", None)),
        check_vma=False,
    )
```

profile of v0, /device:TPU:0, one launch (start us, length us, event | category | flops | bytes accessed | tf_op | source)
XLA Modules:
  0.0 137.9 jit_solution(5644188039326615614)
XLA Ops:
  8.1 3.4 %fusion = f32[16,16]{0,1:T(8,128)S(1)} fusion(f32[16,16,3600]{2,1,0:T(8,128)} %param.6, f32[3600]{0:T(1024)} %param.7), kind=kLoop, calls=%fused_computation.9 | loop fusion | flops 1842944 | bytes 3701824 | tf_op jit(solution)/shard_map/reduce_sum | solution.py:29
  11.5 1.2 multiply_reduce_fusion.1
  12.8 1.7 %multiply_convert_fusion.1 = bf16[16,16,3600]{2,0,1:T(8,128)(2,1)S(1)} fusion(f32[16,16,3600]{2,1,0:T(8,128)S(1)} %copy-done, f32[16,16]{0,1:T(8,128)S(1)} %add_rsqrt_fusion.1, f32[16,16]{0,1:T(8,128)S(1)} %broadcast_multiply_fusion.1, f32[3600]{0:T(1024)S(1)} %copy-done.2), kind=kLoop, calls=%fused_computation.5 | loop fusion | flops 3686400 | bytes 5546048 | tf_op jit(solution)/shard_map/convert_element_type | solution.py:30
  14.5 4.9 %collective-permute-start = (bf16[16,1,3600]{2,0,1:T(8,128)(2,1)S(1)}, bf16[16,1,3600]{2,0,1:T(8,128)(2,1)S(1)}, u32[]{:S(2)}, u32[]{:S(2)}) collective-permute-start(bf16[16,1,3600]{2,0,1:T(8,128)(2,1)S(1)} %get-tuple-element.8), channel_id=1, source_target_pairs={{0,8},{8,16},{16,24},{1,9},{9,17},{17,25},{2,10},{10,18},{18,26},{... | collective-permute-start | bytes 345608 | tf_op jit(solution)/shard_map/ppermute | solution.py:14
  19.4 1.3 collective-permute-start.1
  20.8 0.5 convert_reduce_fusion
  21.2 0.5 fusion.3
  21.7 0.1 collective-permute-done
  21.9 4.3 %collective-permute-done.1 = bf16[16,1,3600]{2,0,1:T(8,128)(2,1)S(1)} collective-permute-done((bf16[16,1,3600]{2,0,1:T(8,128)(2,1)S(1)}, bf16[16,1,3600]{2,0,1:T(8,128)(2,1)S(1)}, u32[]{:S(2)}, u32[]{:S(2)}) %collective-permute-start.1) | collective-permute-done | bytes 115232 | tf_op jit(solution)/shard_map/ppermute | solution.py:17
  26.1 0.4 pad_maximum_fusion.5
  26.6 1.3 collective-permute-start.2
  27.9 0.7 copy.20
  28.6 1.3 collective-permute-start.3
  29.9 0.1 eq.51
  30.1 0.1 select_reduce_fusion
  30.2 0.2 copy.19
  30.4 3.6 %collective-permute-done.3 = bf16[1,18,3600]{2,1,0:T(8,128)(2,1)} collective-permute-done((bf16[1,18,3600]{2,1,0:T(8,128)(2,1)}, bf16[1,18,3600]{2,1,0:T(8,128)(2,1)}, u32[]{:S(2)}, u32[]{:S(2)}) %collective-permute-start.3) | collective-permute-done | bytes 129632 | tf_op jit(solution)/shard_map/ppermute | solution.py:17
  34.0 1.1 copy.21
  35.1 2.9 %maximum_maximum_fusion = (bf16[17,18,3600]{2,0,1:T(8,128)(2,1)S(1)}, bf16[17,18,3600]{2,0,1:T(8,128)(2,1)S(1)}) fusion(bf16[16,1,3600]{2,0,1:T(8,128)(2,1)S(1)} %collective-permute-done.1, bf16[16,16,3600]{2,0,1:T(8,128)(2,1)S(1)} %multiply_convert_fusion.1, bf16[16,1,3600]{2,0,1:T(8,128)(2,1)S(1)} %collective-permute-done, ...), kind=kLoop, calls=%fused_computation.7 | loop fusion | flops 17625600 | bytes 6739200 | tf_op jit(solution)/shard_map/concatenate | solution.py:18
  38.0 4.5 %multiply_reduce_fusion = (f32[16,16]{0,1:T(8,128)S(1)}, f32[16,16,3600]{2,0,1:T(8,128)S(1)}) fusion(bf16[17,18,3600]{2,0,1:T(8,128)(2,1)S(1)} %get-tuple-element.5, bf16[16,1,3600]{2,0,1:T(8,128)(2,1)S(1)} %collective-permute-done.1, bf16[16,16,3600]{2,0,1:T(8,128)(2,1)S(1)} %multiply_convert_fusion.1, bf16[16,1,3600]{2,0,1:T(8,128)(2,1)S(1)} %collective-permute-done, ...), kind=kLoop, calls=%fused_computation.3 | loop fusion | flops 19353344 | bytes 16820224 | tf_op jit(solution)/shard_map/reduce_sum | solution.py:23
  42.5 0.3 multiply_convert_fusion
  42.8 0.3 copy.22
  43.1 1.3 convolution_convert_fusion
  44.5 1.2 fusion.4
  45.7 0.6 dynamic-slice
  46.9 54.2 %all-reduce.3.cloned.1.call-done = bf16[32,3600]{1,0:T(8,128)(2,1)} async-done(((bf16[32,3600]{1,0:T(8,128)(2,1)}), bf16[32,3600]{1,0:T(8,128)(2,1)}) %all-reduce.3.cloned.1.call-update) | async-done | bytes 230416
  101.1 0.8 dynamic-slice_convert_fusion
  101.9 23.7 %psum.7 = f32[4,3600]{1,0:T(4,128)S(1)} all-reduce(f32[4,3600]{1,0:T(4,128)S(1)} %dynamic-slice_convert_fusion), channel_id=1, replica_groups=mesh['dict'=4,'scan'=8] {'dict'}, use_global_device_ids=true, to_apply=%region_8.9 | all-reduce | flops 14400 | bytes 115200 | tf_op jit(solution)/shard_map/psum | solution.py:75
  125.6 0.1 multiply_reduce_fusion.2
  125.8 0.7 broadcast_multiply_fusion
  126.5 3.3 %convolution_reduce_fusion = f32[256]{0:T(256)S(1)} fusion(bf16[256,3600]{1,0:T(8,128)(2,1)S(1)} %bitcast.6, bf16[512,3600]{0,1:T(8,128)(2,1)} %all-gather.2.cloned.1.call-done), kind=kOutput, calls=%fused_computation.18 | convolution fusion | flops 943849216 | bytes 5530624 | tf_op jit(solution)/shard_map/dot_general | solution.py:49
  129.8 0.7 mul.65
  (31 shorter events, 0.4 us)
Async XLA Ops:
  8.0 3.5 %copy-start.2 = (f32[3600]{0:T(1024)S(1)}, f32[3600]{0:T(1024)}, u32[]{:S(2)}) copy-start(f32[3600]{0:T(1024)} %param.7) | copy-start | bytes 43204
  8.0 93.1 %all-reduce.3.cloned.1.call-start = ((), (), s32[]{:S(2)}) async-start(), calls=%async_computation.1 | async-start | bytes 475136
  8.1 3.4 %copy-start = (f32[16,16,3600]{2,1,0:T(8,128)S(1)}, f32[16,16,3600]{2,1,0:T(8,128)}, u32[]{:S(2)}) copy-start(f32[16,16,3600]{2,1,0:T(8,128)} %param.6) | copy-start | bytes 11059204
  12.7 8.0 %copy-start.3 = (s32[16,16]{1,0:T(8,128)S(1)}, s32[16,16]{1,0:T(8,128)}, u32[]{:S(2)}) copy-start(s32[16,16]{1,0:T(8,128)} %param.10) | copy-start | bytes 3076
  12.7 8.0 %copy-start.1 = (bf16[128,3600]{0,1:T(8,128)(2,1)S(1)}, bf16[128,3600]{0,1:T(8,128)(2,1)}, u32[]{:S(2)}) copy-start(bf16[128,3600]{0,1:T(8,128)(2,1)} %param.8) | copy-start | bytes 2764804
  14.4 15.6 %copy-start.4 = (s32[16,16]{1,0:T(8,128)S(1)}, s32[16,16]{1,0:T(8,128)}, u32[]{:S(2)}) copy-start(s32[16,16]{1,0:T(8,128)} %param.9) | copy-start | bytes 3076
  14.4 15.6 %copy-start.5 = (s32[32]{0:T(128)S(1)}, s32[32]{0:T(128)}, u32[]{:S(2)}) copy-start(s32[32]{0:T(128)} %param.11) | copy-start | bytes 388
  14.5 7.4 %collective-permute-start = (bf16[16,1,3600]{2,0,1:T(8,128)(2,1)S(1)}, bf16[16,1,3600]{2,0,1:T(8,128)(2,1)S(1)}, u32[]{:S(2)}, u32[]{:S(2)}) collective-permute-start(bf16[16,1,3600]{2,0,1:T(8,128)(2,1)S(1)} %get-tuple-element.8), channel_id=1, source_target_pairs={{0,8},{8,16},{16,24},{1,9},{9,17},{17,25},{2,10},{10,18},{18,26},{... | collective-permute-start | bytes 345608 | tf_op jit(solution)/shard_map/ppermute | solution.py:14
  19.4 6.7 %collective-permute-start.1 = (bf16[16,1,3600]{2,0,1:T(8,128)(2,1)S(1)}, bf16[16,1,3600]{2,0,1:T(8,128)(2,1)S(1)}, u32[]{:S(2)}, u32[]{:S(2)}) collective-permute-start(bf16[16,1,3600]{2,0,1:T(8,128)(2,1)S(1)} %get-tuple-element.9), channel_id=1, source_target_pairs={{8,0},{16,8},{24,16},{9,1},{17,9},{25,17},{10,2},{18,10},{26,18},{... | collective-permute-start | bytes 345608 | tf_op jit(solution)/shard_map/ppermute | solution.py:17
  26.6 3.6 %collective-permute-start.2 = (bf16[1,18,3600]{2,1,0:T(8,128)(2,1)S(1)}, bf16[1,18,3600]{2,1,0:T(8,128)(2,1)S(1)}, u32[]{:S(2)}, u32[]{:S(2)}) collective-permute-start(bf16[1,18,3600]{2,1,0:T(8,128)(2,1)S(1)} %copy.18), channel_id=1, source_target_pairs={{0,1},{1,2},{2,3},{3,4},{4,5},{5,6},{6,7},{8,9},{9,10},{10,11},{11... | collective-permute-start | bytes 388808 | tf_op jit(solution)/shard_map/ppermute | solution.py:14
  28.6 5.4 %collective-permute-start.3 = (bf16[1,18,3600]{2,1,0:T(8,128)(2,1)}, bf16[1,18,3600]{2,1,0:T(8,128)(2,1)}, u32[]{:S(2)}, u32[]{:S(2)}) collective-permute-start(bf16[1,18,3600]{2,1,0:T(8,128)(2,1)} %copy.20), channel_id=1, source_target_pairs={{1,0},{2,1},{3,2},{4,3},{5,4},{6,5},{7,6},{9,8},{10,9},{11,10},{12... | collective-permute-start | bytes 388808 | tf_op jit(solution)/shard_map/ppermute | solution.py:17
  42.8 2.9 %copy-start.6 = (u32[32]{0:T(128)S(1)}, u32[32]{0:T(128)}, u32[]{:S(2)}) copy-start(u32[32]{0:T(128)} %constant.28) | copy-start | bytes 388
  44.5 82.0 %all-gather.2.cloned.1.call-start = ((), (), s32[]{:S(2)}) async-start(), calls=%async_computation | async-start | bytes 4608000 | tf_op jit(solution)/shard_map/all_gather | solution.py:51
Sparse Core Ops, SparseCore 0:
  44.6 56.4 all-reduce.2
Sparse Core Ops, SparseCore 1:
  46.5 77.8 all-gather.1
where the time goes:
time: 138 us
  waiting for transfers between devices  62.2 us (45%)
  blocking collectives  23.7 us (17%)
  other arithmetic  18.4 us (13%)
  between operations  16.3 us (12%)
  starting transfers between devices  8.89 us (6%)
  matrix products  4.6 us (3%)
  local copies, waits for them, and re-layouts  3.88 us (3%)
    unnamed x3, waiting for transfers between devices  54.2 us
    psum x1, blocking collectives, shards(): grain_total = lax.psum(partial_rows, 'dict')  23.7 us
    ppermute x2, waiting for transfers between devices, with_halo(): lax.ppermute(lax.slice_in_dim(block, 0, width, axis=dim), axis, backward)  7.83 us
    reduce_sum x4, other arithmetic, unit_rows(): mean_square = jnp.mean(values * values, axis=-1, keepdims=True)  6.35 us
    ppermute x2, starting transfers between devices, with_halo(): lax.ppermute(lax.slice_in_dim(block, block.shape[dim] - width, None, axis...  6.24 us
    reduce_sum x1, other arithmetic, filter_points(): centered = centered - jnp.mean(centered, axis=-1, keepdims=True)  3.38 us
    dot_general x1, matrix products, shards(): lax.dot_general(indexed, lax.all_gather(unit_panel, 'dict', axis=0, tiled...  3.3 us
    concatenate x1, other arithmetic, with_halo(): block = jnp.concatenate([low, block, high], axis=dim)  2.85 us
  transfers between devices with their start and end apart: 6, of which 4 were waited for; matrix products, arithmetic and copies ran while one was open for 4% of the time, Pallas kernels for 0%

commit v1 on v0

v1 whole, which is shorter than its diff:
```python
import functools

import jax
import jax.numpy as jnp
from jax import lax
from jax.experimental import pallas as pl
from jax.experimental.pallas import tpu as pltpu
from jax.sharding import PartitionSpec as P

MESH = pl.DeviceIdType.MESH
EPS = 1e-05
GROUP = 8
F32 = jnp.float32
BF16 = jnp.bfloat16


def iota(shape, dim):
    return lax.broadcasted_iota(jnp.int32, shape, dim)


def near(a, b):
    return (a - b <= 1) & (b - a <= 1)


def unit(values, pixels):
    square = jnp.sum(values * values, axis=-1, keepdims=True) * (1.0 / pixels)
    return values * lax.rsqrt(square + EPS)


def centred(values, pixels):
    return values - jnp.sum(values, axis=-1, keepdims=True) * (1.0 / pixels)


def kernel(
    D, S, G, TR, TC, pix, R,
    patterns, templates, background, grain_id, keep_mask, grain_row,
    score_out, grain_out,
    pat, raw, filt, near_mat, pick_mat, halo_mat, sel_mat,
    edge, corner_src, corner_dst, halo, neigh, indexed, panel,
    gsum, grecv, zbuf, best,
    pat_sem, raw_sem, zsend, nsend, trecv, hsend, hrecv,
    gsend, grecv_sem, zgsend, zgrecv,
):
    z = lax.axis_index("dict")
    s = lax.axis_index("scan")
    points = TR * TC
    rows_out = G // S
    cuts = [(a, min(a + 512, pix)) for a in range(0, pix, 512)]

    def pat_copy(i):
        return pltpu.make_async_copy(patterns.at[i], pat.at[i], pat_sem.at[i])

    raw_copy = pltpu.make_async_copy(templates, raw, raw_sem)
    raw_copy.start()
    for i in range(TR):
        pat_copy(i).start()

    halo[...] = jnp.zeros_like(halo)

    barrier = pltpu.get_barrier_semaphore()

    def hello(zz, ss):
        pl.semaphore_signal(
            barrier, inc=1, device_id={"dict": zz, "scan": ss}, device_id_type=MESH
        )

    for k in range(1, S):
        hello(z, lax.rem(s + k, S))
    for k in range(1, D):
        hello(lax.rem(z + k, D), s)
    diagonals = [(-1, -1), (-1, 1), (1, -1), (1, 1)]

    def inside(ds, dz):
        ok = None
        for cond in (
            [s >= 1] if ds < 0 else [s <= S - 2] if ds > 0 else []
        ) + ([z >= 1] if dz < 0 else [z <= D - 2] if dz > 0 else []):
            ok = cond if ok is None else ok & cond
        return ok

    for ds, dz in diagonals:
        @pl.when(inside(ds, dz))
        def _():
            hello(z + dz, s + ds)

    p0, q1 = iota((points, points), 0), iota((points, points), 1)
    near_mat[...] = jnp.where(
        near(p0 // TC, q1 // TC) & near(p0 % TC, q1 % TC), 1.0, 0.0
    ).astype(BF16)
    i0, q = iota((48, points), 0), iota((48, points), 1)
    k0 = (i0 - 32) // 2
    corner_at = jnp.where(
        k0 == 0, 0, jnp.where(k0 == 1, TC - 1, jnp.where(k0 == 2, points - TC, points - 1))
    )
    want = jnp.where(
        i0 < 16, i0 * TC, jnp.where(i0 < 32, (i0 - 16) * TC + TC - 1,
                                    jnp.where(i0 < 40, corner_at, -1))
    )
    pick_mat[...] = jnp.where(q == want, 1.0, 0.0).astype(BF16)
    p, h = iota((points, 128), 0), iota((points, 128), 1)
    slot, i = h // 16, h % 16
    r, c = p // TC, p % TC
    side = (
        ((slot == 0) & (r == 0) & near(c, i))
        | ((slot == 1) & (r == TR - 1) & near(c, i))
        | ((slot == 2) & (c == 0) & near(r, i))
        | ((slot == 3) & (c == TC - 1) & near(r, i))
        | ((slot == 4) & (i == 0) & (p == 0))
        | ((slot == 5) & (i == 0) & (p == TC - 1))
        | ((slot == 6) & (i == 0) & (p == points - TC))
        | ((slot == 7) & (i == 0) & (p == points - 1))
    )
    halo_mat[...] = jnp.where(side, 1.0, 0.0).astype(BF16)
    code = jnp.where(keep_mask[...] == 1, grain_id[...], -1).astype(F32).astype(BF16)
    spread = jnp.where(iota((TC, points), 1) % TC == iota((TC, points), 0), 1.0, 0.0).astype(BF16)
    wide = jnp.dot(code, spread, preferred_element_type=F32)
    own = iota((TR, points), 1) // TC == iota((TR, points), 0)
    code_row = jnp.sum(jnp.where(own, wide, 0.0), axis=0, keepdims=True)
    one_hot = jnp.where(
        iota((G, points), 0).astype(F32) == code_row, 1.0, 0.0
    ).astype(BF16)
    to_row = jnp.where(iota((G, G), 0) == grain_row[...], 1.0, 0.0).astype(BF16)
    sel_mat[...] = jnp.dot(to_row, one_hot, preferred_element_type=F32).astype(BF16)

    piece = lax.rem(s, GROUP)
    base = s - piece
    core = lax.rem(piece, 2)
    xbit = lax.rem(piece // 2, 2)
    ybit = piece // 4
    px, py = piece + 2 - 4 * xbit, piece + 4 - 8 * ybit
    first = jnp.where(core == 0, px, py)
    second = jnp.where(core == 0, py, px)
    twin = 1 - 2 * core
    across = first + second - piece

    def remote(src, dst, ssem, rsem, zz, ss):
        return pltpu.make_async_remote_copy(
            src_ref=src, dst_ref=dst, send_sem=ssem, recv_sem=rsem,
            device_id={"dict": zz, "scan": ss}, device_id_type=MESH,
        )

    def shard_copy(d, q, ssem, zz, ss):
        return remote(panel.at[d, q], panel.at[d, q], ssem, trecv.at[d, q], zz, ss)

    def z_copy(d, sem_at, zz):
        return shard_copy(d, piece, zsend.at[sem_at], zz, s)

    def normalise(j):
        panel[z, j] = unit(centred(raw[j].astype(F32), pix), pix).astype(BF16)

    near_end = jnp.minimum(z, D - 1 - z)

    def event_shard(e):
        paired = e <= 2 * near_end
        k = jnp.where(paired, (e + 1) // 2, e - near_end)
        lower = jnp.where(paired, e % 2 == 1, z > near_end)
        return jnp.where(lower, z - k, z + k)

    def relay(d):
        target = jnp.where(d < z, z + 1, z - 1)
        return (target >= 0) & (target < D), target

    def piece_sends(d):
        return [
            (piece, 0, first), (piece, 1, second), (piece, 2, piece + twin),
            (first, 3, second), (first, 4, piece + twin),
            (second, 5, piece + twin), (across, 6, piece + twin),
        ]

    def in_plane(d, which):
        q, k, to = piece_sends(d)[which]
        return shard_copy(d, q, nsend.at[d, k], z, base + to)

    def arrived(d, q):
        shard_copy(d, q, nsend.at[d, 0], z, base + first).wait_recv()

    def stage_a(e):
        d = event_shard(e)
        arrived(d, piece)
        on, target = relay(d)

        @pl.when(on)
        def _():
            z_copy(d, d, target).start()

        for which in (0, 1, 2):
            in_plane(d, which).start()

    def stage_b(e):
        d = event_shard(e)
        arrived(d, first)
        for which in (3, 4):
            in_plane(d, which).start()

    def stage_c(e):
        d = event_shard(e)
        arrived(d, second)
        in_plane(d, 5).start()
        arrived(d, across)
        in_plane(d, 6).start()

    def score(d):
        dots = lax.dot_general(
            panel[d].reshape(R, pix), indexed[...], (((1,), (1,)), ((), ())),
            preferred_element_type=F32,
        )
        best[...] = jnp.maximum(best[...], jnp.max(dots, axis=0, keepdims=True))

    def stage_d(e):
        d = event_shard(e)
        for q in (piece, first, second, across):
            arrived(d, q + twin)
        score(d)

    def stage_end(e):
        d = event_shard(e)
        on, target = relay(d)

        @pl.when(on)
        def _():
            z_copy(d, d, target).wait_send()

        for which in range(7):
            in_plane(d, which).wait_send()

    halo_moves = [
        (filt.at[TR - 1], halo.at[0], 1, 0),
        (filt.at[0], halo.at[1], -1, 0),
        (edge.at[1], halo.at[2], 0, 1),
        (edge.at[0], halo.at[3], 0, -1),
        (corner_src.at[3], corner_dst.at[0], 1, 1),
        (corner_src.at[2], corner_dst.at[1], 1, -1),
        (corner_src.at[1], corner_dst.at[2], -1, 1),
        (corner_src.at[0], corner_dst.at[3], -1, -1),
    ]

    def halo_copy(k):
        src, dst, ds, dz = halo_moves[k]
        return remote(src, dst, hsend.at[k], hrecv.at[k], z + dz, s + ds)

    def halo_send(k):
        @pl.when(inside(halo_moves[k][2], halo_moves[k][3]))
        def _():
            halo_copy(k).start()

    diag_count = sum(
        [jnp.where(inside(ds, dz), 1, 0) for ds, dz in diagonals]
    )
    pl.semaphore_wait(barrier, S - 1 + D - 1 + diag_count)

    raw_copy.wait()
    normalise(piece)

    @pl.when(z < D - 1)
    def _():
        z_copy(z, z, z + 1).start()

    @pl.when(z > 0)
    def _():
        z_copy(z, D, z - 1).start()

    def filter_row(i):
        centre = centred(pat[i] - background[...], pix)
        filt[i] = unit(centre, pix).astype(BF16)

    for i in range(TR):
        pat_copy(i).wait()
    filter_row(TR - 1)
    halo_send(0)
    filter_row(0)
    halo_send(1)

    @pl.loop(1, TR - 1)
    def _(i):
        filter_row(i)

    for a, b in cuts:
        got = jnp.dot(
            pick_mat[...], filt[:, :, a:b].reshape(points, b - a), preferred_element_type=F32
        ).astype(BF16)
        edge[0, :, a:b] = got[0:16]
        edge[1, :, a:b] = got[16:32]
        for k in range(4):
            corner_src[k, :, a:b] = got[32 + 2 * k : 34 + 2 * k]
    for k in range(2, 8):
        halo_send(k)

    events = min(D - 1, 3)
    stage_a(1)

    for j in range(1, GROUP):
        normalise(lax.rem(piece + j, GROUP))

    for a, b in cuts:
        neigh[:, a:b] = jnp.dot(
            near_mat[...], filt[:, :, a:b].reshape(points, b - a), preferred_element_type=F32
        )
    stage_b(1)
    if events >= 2:
        stage_a(2)

    for k in range(8):
        ds, dz = halo_moves[k][2], halo_moves[k][3]

        @pl.when(inside(-ds, -dz))
        def _():
            halo_copy(k).wait_recv()
            if k >= 4:
                halo[k, 0:2, :] = corner_dst[k - 4]

    total = jnp.zeros((points, 1), F32)
    for a, b in cuts:
        part = neigh[:, a:b] + jnp.dot(
            halo_mat[...], halo[:, :, a:b].reshape(128, b - a), preferred_element_type=F32
        )
        neigh[:, a:b] = part
        total = total + jnp.sum(part * part, axis=1, keepdims=True)
    scale = lax.rsqrt(total * (1.0 / pix) + EPS)
    for a, b in cuts:
        indexed[:, a:b] = (neigh[:, a:b] * scale).astype(BF16)

    for a, b in cuts:
        sums = jnp.dot(sel_mat[...], indexed[:, a:b], preferred_element_type=F32).astype(BF16)
        for k in range(S):
            gsum[k, :, a:b] = sums[k * rows_out : (k + 1) * rows_out]

    def grain_copy(to):
        return remote(gsum.at[to], grecv.at[s], gsend.at[to], grecv_sem.at[s], z, to)

    for k in range(1, S):
        grain_copy(lax.rem(s + k, S)).start()

    stage_c(1)
    if events >= 2:
        stage_b(2)
    if events >= 3:
        stage_a(3)
    best[...] = jnp.full_like(best, -1e30)
    score(z)

    for k in range(1, S):
        source = lax.rem(s + k, S)
        remote(
            gsum.at[source], grecv.at[source], gsend.at[source], grecv_sem.at[source], z, source
        ).wait_recv()
    grecv[s] = gsum[s]
    held = jnp.zeros((rows_out, pix), F32)
    for k in range(S):
        held = held + grecv[k].astype(F32)
    zbuf[z] = held.astype(BF16)

    def z_grain(to, at):
        return remote(zbuf.at[at], zbuf.at[at], zgsend.at[to], zgrecv.at[at], to, s)

    for k in range(1, D):
        z_grain(lax.rem(z + k, D), z).start()

    if events >= 2:
        stage_c(2)
    if events >= 3:
        stage_b(3)
    stage_d(1)
    if events >= 2:
        stage_d(2)

    for k in range(1, D):
        source = lax.rem(z + k, D)
        z_grain(source, source).wait_recv()
    held = jnp.zeros((rows_out, pix), F32)
    for k in range(D):
        held = held + zbuf[k].astype(F32)
    grain_out[...] = unit(held, pix)

    if events >= 3:
        stage_c(3)
        stage_d(3)
    if D > 4:
        @pl.loop(4, D)
        def _(e):
            stage_a(e)
            stage_b(e)
            stage_c(e)
            stage_d(e)

    score_row = best[...] * (1.0 / pix**0.5)
    for k in range(TR):
        score_out[k : k + 1, :] = score_row[:, k * TC : (k + 1) * TC]

    @pl.when(z < D - 1)
    def _():
        z_copy(z, z, z + 1).wait_send()

    @pl.when(z > 0)
    def _():
        z_copy(z, D, z - 1).wait_send()

    @pl.loop(1, D)
    def _(e):
        stage_end(e)

    for k in range(8):
        @pl.when(inside(halo_moves[k][2], halo_moves[k][3]))
        def _():
            halo_copy(k).wait_send()

    for k in range(1, S):
        grain_copy(lax.rem(s + k, S)).wait_send()
    for k in range(1, D):
        z_grain(lax.rem(z + k, D), z).wait_send()


def shards(D, S, patterns, background, templates, grain_id, keep_mask, grain_row):
    TR, TC, pix = patterns.shape
    R = templates.shape[0]
    G = grain_row.shape[0]
    rows_out = G // S
    points = TR * TC
    each = R // GROUP
    dma = pltpu.SemaphoreType.DMA
    vmem = pl.BlockSpec(memory_space=pltpu.VMEM)
    anywhere = pl.BlockSpec(memory_space=pl.ANY)
    return pl.pallas_call(
        functools.partial(kernel, D, S, G, TR, TC, pix, R),
        out_shape=(
            jax.ShapeDtypeStruct((TR, TC), F32),
            jax.ShapeDtypeStruct((rows_out, pix), F32),
        ),
        in_specs=[anywhere, anywhere, vmem, vmem, vmem, vmem],
        out_specs=(vmem, vmem),
        scratch_shapes=[
            pltpu.VMEM((TR, TC, pix), F32),
            pltpu.VMEM((GROUP, each, pix), BF16),
            pltpu.VMEM((TR, TC, pix), BF16),
            pltpu.VMEM((points, points), BF16),
            pltpu.VMEM((48, points), BF16),
            pltpu.VMEM((points, 128), BF16),
            pltpu.VMEM((G, points), BF16),
            pltpu.VMEM((2, 16, pix), BF16),
            pltpu.VMEM((4, 2, pix), BF16),
            pltpu.VMEM((4, 2, pix), BF16),
            pltpu.VMEM((8, 16, pix), BF16),
            pltpu.VMEM((points, pix), F32),
            pltpu.VMEM((points, pix), BF16),
            pltpu.VMEM((D, GROUP, each, pix), BF16),
            pltpu.VMEM((S, rows_out, pix), BF16),
            pltpu.VMEM((S, rows_out, pix), BF16),
            pltpu.VMEM((D, rows_out, pix), BF16),
            pltpu.VMEM((1, points), F32),
            dma((TR,)),
            dma,
            dma((D + 1,)),
            dma((D, 7)),
            dma((D, GROUP)),
            dma((8,)),
            dma((8,)),
            dma((S,)),
            dma((S,)),
            dma((D,)),
            dma((D,)),
        ],
        compiler_params=pltpu.CompilerParams(
            collective_id=0, has_side_effects=True, vmem_limit_bytes=56 * 1024 * 1024
        ),
    )(
        patterns,
        templates.reshape(GROUP, each, pix),
        background.reshape(1, pix),
        grain_id,
        keep_mask,
        grain_row.reshape(1, G),
    )


def solution(mesh):
    D, S = mesh.shape["dict"], mesh.shape["scan"]
    return jax.shard_map(
        functools.partial(shards, D, S),
        mesh=mesh,
        in_specs=(
            P("scan", "dict", None),
            P(),
            P("dict", None),
            P("scan", "dict"),
            P("scan", "dict"),
            P(),
        ),
        out_specs=(P("scan", "dict"), P("scan", None)),
        check_vma=False,
    )
```

time: 138 us -> 43.7 us (0.32)
  the two profiles are of different devices: /device:TPU:0 before, /device:TPU:1 now
where the time goes in v1:
time: 43.7 us; the launch traced here: 43.3 us
  Pallas kernels  36.3 us (83%)
  local copies, waits for them, and re-layouts  6.35 us (15%)
  between operations  0.64 us (1%)
    pallas_call x1, Pallas kernels, shards(): pl.pallas_call(functools.partial(kernel, D, S, G, TR, TC, pix, R), out_sh...  36.3 us
    unnamed x3, local copies, waits for them, and re-layouts  5.02 us
    reshape x1, local copies, waits for them, and re-layouts, shards(): background.reshape(1, pix)  1.33 us

profile of v1, /device:TPU:1, one launch (start us, length us, event | category | flops | bytes accessed | tf_op | source)
XLA Modules:
  0.0 43.3 jit_solution(14955852970428255397)
XLA Ops:
  0.6 1.3 %reshape.14.background = f32[1,3600]{1,0:T(1,128)} reshape(f32[3600]{0:T(1024)} %param.7) | data formatting | bytes 28800 | tf_op jit(solution)/shard_map/reshape | solution.py:467
  2.0 2.3 %copy.8 = bf16[128,3600]{1,0:T(8,128)(2,1)} copy(bf16[128,3600]{0,1:T(8,128)(2,1)} %param.8) | data formatting | bytes 1843200 | tf_op args[2]
  4.2 36.3 %shard_map.77 = (f32[16,16]{1,0:T(8,128)}, f32[4,3600]{1,0:T(4,128)}) custom-call(f32[16,16,3600]{2,1,0:T(8,128)} %patterns.1, bf16[8,16,3600]{2,1,0:T(8,128)(2,1)} %bitcast.2, f32[1,3600]{1,0:T(1,128)} %reshape.14.background, s32[16,16]{1,0:T(8,128)} %grain_id.1, s32[16,16]{1,0:T(8,128)} %keep_mask.1, s32[1,32]{1,0:T(1,128)} %bitcast.3), custom_call_target="tpu_custom_call" | custom-call | tf_op jit(solution)/shard_map/pallas_call | solution.py:422
  40.6 1.3 %copy.11 = f32[16,16]{1,0:T(8,128)} copy(f32[16,16]{1,0:T(8,128)} %get-tuple-element.4) | data formatting | bytes 2048
  41.9 1.5 %copy.12 = f32[4,3600]{1,0:T(4,128)} copy(f32[4,3600]{1,0:T(4,128)} %get-tuple-element.5) | data formatting | bytes 115200

commit v2 on v1

--- a/solution.py
+++ b/solution.py
@@ -35,16 +35,18 @@
     D, S, G, TR, TC, pix, R,
     patterns, templates, background, grain_id, keep_mask, grain_row,
     score_out, grain_out,
-    pat, raw, filt, near_mat, pick_mat, halo_mat, sel_mat,
+    pat, raw, ground, filt, near_mat, pick_mat, halo_mat, sel_mat,
     edge, corner_src, corner_dst, halo, neigh, indexed, panel,
     gsum, grecv, zbuf, best,
-    pat_sem, raw_sem, zsend, nsend, trecv, hsend, hrecv,
+    pat_sem, raw_sem, ground_sem, zsend, nsend, trecv, hsend, hrecv,
     gsend, grecv_sem, zgsend, zgrecv,
 ):
     z = lax.axis_index("dict")
     s = lax.axis_index("scan")
     points = TR * TC
     rows_out = G // S
+    run = panel.shape[2]
+    wide_pix = run * GROUP
     cuts = [(a, min(a + 512, pix)) for a in range(0, pix, 512)]
 
     def pat_copy(i):
@@ -52,10 +54,14 @@
 
     raw_copy = pltpu.make_async_copy(templates, raw, raw_sem)
     raw_copy.start()
-    for i in range(TR):
+    ground_copy = pltpu.make_async_copy(background, ground.at[0], ground_sem)
+    ground_copy.start()
+    for i in [TR - 1] + list(range(TR - 1)):
         pat_copy(i).start()
 
     halo[...] = jnp.zeros_like(halo)
+    tail = pix // 128 * 128
+    indexed[:, tail:] = jnp.zeros((points, wide_pix - tail), BF16)
 
     barrier = pltpu.get_barrier_semaphore()
 
@@ -83,12 +89,13 @@
         def _():
             hello(z + dz, s + ds)
 
+    bits, low = TC.bit_length() - 1, TC - 1
     p0, q1 = iota((points, points), 0), iota((points, points), 1)
     near_mat[...] = jnp.where(
-        near(p0 // TC, q1 // TC) & near(p0 % TC, q1 % TC), 1.0, 0.0
+        near(p0 >> bits, q1 >> bits) & near(p0 & low, q1 & low), 1.0, 0.0
     ).astype(BF16)
     i0, q = iota((48, points), 0), iota((48, points), 1)
-    k0 = (i0 - 32) // 2
+    k0 = (i0 - 32) >> 1
     corner_at = jnp.where(
         k0 == 0, 0, jnp.where(k0 == 1, TC - 1, jnp.where(k0 == 2, points - TC, points - 1))
     )
@@ -98,8 +105,8 @@
     )
     pick_mat[...] = jnp.where(q == want, 1.0, 0.0).astype(BF16)
     p, h = iota((points, 128), 0), iota((points, 128), 1)
-    slot, i = h // 16, h % 16
-    r, c = p // TC, p % TC
+    slot, i = h >> 4, h & 15
+    r, c = p >> bits, p & low
     side = (
         ((slot == 0) & (r == 0) & near(c, i))
         | ((slot == 1) & (r == TR - 1) & near(c, i))
@@ -112,9 +119,9 @@
     )
     halo_mat[...] = jnp.where(side, 1.0, 0.0).astype(BF16)
     code = jnp.where(keep_mask[...] == 1, grain_id[...], -1).astype(F32).astype(BF16)
-    spread = jnp.where(iota((TC, points), 1) % TC == iota((TC, points), 0), 1.0, 0.0).astype(BF16)
+    spread = jnp.where((iota((TC, points), 1) & low) == iota((TC, points), 0), 1.0, 0.0).astype(BF16)
     wide = jnp.dot(code, spread, preferred_element_type=F32)
-    own = iota((TR, points), 1) // TC == iota((TR, points), 0)
+    own = (iota((TR, points), 1) >> bits) == iota((TR, points), 0)
     code_row = jnp.sum(jnp.where(own, wide, 0.0), axis=0, keepdims=True)
     one_hot = jnp.where(
         iota((G, points), 0).astype(F32) == code_row, 1.0, 0.0
@@ -145,8 +152,16 @@
     def z_copy(d, sem_at, zz):
         return shard_copy(d, piece, zsend.at[sem_at], zz, s)
 
-    def normalise(j):
-        panel[z, j] = unit(centred(raw[j].astype(F32), pix), pix).astype(BF16)
+    def normalise():
+        mean = jnp.sum(raw[...].astype(F32), axis=0, keepdims=True) * (1.0 / pix)
+        off = raw[...].astype(F32) - mean
+        square = jnp.sum(off * off, axis=0, keepdims=True) * (1.0 / pix)
+        gain = lax.rsqrt(square + EPS)
+        for j in range(GROUP):
+            a, b = j * run, min((j + 1) * run, pix)
+            panel[z, j, 0 : b - a, :] = ((raw[a:b, :].astype(F32) - mean) * gain).astype(BF16)
+            if b - a < run:
+                panel[z, j, b - a : run, :] = jnp.zeros((run - b + a, R), BF16)
 
     near_end = jnp.minimum(z, D - 1 - z)
 
@@ -200,11 +215,10 @@
         in_plane(d, 6).start()
 
     def score(d):
-        dots = lax.dot_general(
-            panel[d].reshape(R, pix), indexed[...], (((1,), (1,)), ((), ())),
-            preferred_element_type=F32,
+        dots = jnp.dot(
+            indexed[...], panel[d].reshape(wide_pix, R), preferred_element_type=F32
         )
-        best[...] = jnp.maximum(best[...], jnp.max(dots, axis=0, keepdims=True))
+        best[...] = jnp.maximum(best[...], dots)
 
     def stage_d(e):
         d = event_shard(e)
@@ -246,10 +260,10 @@
     diag_count = sum(
         [jnp.where(inside(ds, dz), 1, 0) for ds, dz in diagonals]
     )
+    raw_copy.wait()
+    normalise()
     pl.semaphore_wait(barrier, S - 1 + D - 1 + diag_count)
 
-    raw_copy.wait()
-    normalise(piece)
 
     @pl.when(z < D - 1)
     def _():
@@ -259,20 +273,19 @@
     def _():
         z_copy(z, D, z - 1).start()
 
-    def filter_row(i):
-        centre = centred(pat[i] - background[...], pix)
-        filt[i] = unit(centre, pix).astype(BF16)
-
-    for i in range(TR):
-        pat_copy(i).wait()
-    filter_row(TR - 1)
+    def filter_rows(a, b):
+        for i in range(a, b):
+            pat_copy(i).wait()
+        centre = centred(pat[a:b] - ground[...].reshape(1, 1, pix), pix)
+        filt[a:b] = unit(centre, pix).astype(BF16)
+
+    ground_copy.wait()
+    filter_rows(TR - 1, TR)
     halo_send(0)
-    filter_row(0)
+    filter_rows(0, 1)
     halo_send(1)
-
-    @pl.loop(1, TR - 1)
-    def _(i):
-        filter_row(i)
+    for a in range(1, TR - 1, 7):
+        filter_rows(a, min(a + 7, TR - 1))
 
     for a, b in cuts:
         got = jnp.dot(
@@ -288,9 +301,6 @@
     events = min(D - 1, 3)
     stage_a(1)
 
-    for j in range(1, GROUP):
-        normalise(lax.rem(piece + j, GROUP))
-
     for a, b in cuts:
         neigh[:, a:b] = jnp.dot(
             near_mat[...], filt[:, :, a:b].reshape(points, b - a), preferred_element_type=F32
@@ -382,7 +392,7 @@
             stage_c(e)
             stage_d(e)
 
-    score_row = best[...] * (1.0 / pix**0.5)
+    score_row = jnp.max(best[...].T, axis=0, keepdims=True) * (1.0 / pix**0.5)
     for k in range(TR):
         score_out[k : k + 1, :] = score_row[:, k * TC : (k + 1) * TC]
 
@@ -407,6 +417,11 @@
         grain_copy(lax.rem(s + k, S)).wait_send()
     for k in range(1, D):
         z_grain(lax.rem(z + k, D), z).wait_send()
+
+
+def hand_over(found, sums, score_out, grain_out):
+    score_out[...] = found[...]
+    grain_out[...] = sums[...]
 
 
 def shards(D, S, patterns, background, templates, grain_id, keep_mask, grain_row):
@@ -415,21 +430,22 @@
     G = grain_row.shape[0]
     rows_out = G // S
     points = TR * TC
-    each = R // GROUP
+    run = -(-pix // (GROUP * 16)) * 16
     dma = pltpu.SemaphoreType.DMA
     vmem = pl.BlockSpec(memory_space=pltpu.VMEM)
     anywhere = pl.BlockSpec(memory_space=pl.ANY)
-    return pl.pallas_call(
+    found, sums = pl.pallas_call(
         functools.partial(kernel, D, S, G, TR, TC, pix, R),
         out_shape=(
             jax.ShapeDtypeStruct((TR, TC), F32),
             jax.ShapeDtypeStruct((rows_out, pix), F32),
         ),
-        in_specs=[anywhere, anywhere, vmem, vmem, vmem, vmem],
+        in_specs=[anywhere, anywhere, anywhere, vmem, vmem, vmem],
         out_specs=(vmem, vmem),
         scratch_shapes=[
             pltpu.VMEM((TR, TC, pix), F32),
-            pltpu.VMEM((GROUP, each, pix), BF16),
+            pltpu.VMEM((pix, R), BF16),
+            pltpu.VMEM((1, pix), F32),
             pltpu.VMEM((TR, TC, pix), BF16),
             pltpu.VMEM((points, points), BF16),
             pltpu.VMEM((48, points), BF16),
@@ -440,13 +456,14 @@
             pltpu.VMEM((4, 2, pix), BF16),
             pltpu.VMEM((8, 16, pix), BF16),
             pltpu.VMEM((points, pix), F32),
-            pltpu.VMEM((points, pix), BF16),
-            pltpu.VMEM((D, GROUP, each, pix), BF16),
+            pltpu.VMEM((points, run * GROUP), BF16),
+            pltpu.VMEM((D, GROUP, run, R), BF16),
             pltpu.VMEM((S, rows_out, pix), BF16),
             pltpu.VMEM((S, rows_out, pix), BF16),
             pltpu.VMEM((D, rows_out, pix), BF16),
-            pltpu.VMEM((1, points), F32),
+            pltpu.VMEM((points, R), F32),
             dma((TR,)),
+            dma,
             dma,
             dma((D + 1,)),
             dma((D, 7)),
@@ -463,12 +480,21 @@
         ),
     )(
         patterns,
-        templates.reshape(GROUP, each, pix),
-        background.reshape(1, pix),
+        templates.T,
+        background,
         grain_id,
         keep_mask,
         grain_row.reshape(1, G),
     )
+    return pl.pallas_call(
+        hand_over,
+        out_shape=(
+            jax.ShapeDtypeStruct(found.shape, F32),
+            jax.ShapeDtypeStruct(sums.shape, F32),
+        ),
+        in_specs=[vmem, vmem],
+        out_specs=(vmem, vmem),
+    )(found, sums)
 
 
 def solution(mesh):

time: 43.7 us -> 40.3 us (0.922)
  local copies, waits for them, and re-layouts: 6.35 us -> 0 us
  Pallas kernels: 36.3 us -> 39.5 us
    unnamed x3 -> x0, local copies, waits for them, and re-layouts: 5.02 us -> none
    pallas_call x1, Pallas kernels: 36.3 us -> 38 us  [shards(): pl.pallas_call(functools.partial(kernel, D, S, G, TR, TC, pix, R), out_sh...]
    pallas_call x0 -> x1, Pallas kernels: none -> 1.47 us  [shards(): pl.pallas_call(hand_over, out_shape=(jax.ShapeDtypeStruct(found.shape, F3...]
    reshape x1 -> x0, local copies, waits for them, and re-layouts: 1.33 us -> none  [shards(): background.reshape(1, pix)]
where the time goes in v2:
time: 40.3 us; the launch traced here: 40.1 us
  Pallas kernels  39.5 us (98%)
  between operations  0.64 us (2%)
    pallas_call x1, Pallas kernels, shards(): pl.pallas_call(functools.partial(kernel, D, S, G, TR, TC, pix, R), out_sh...  38 us
    pallas_call x1, Pallas kernels, shards(): pl.pallas_call(hand_over, out_shape=(jax.ShapeDtypeStruct(found.shape, F3...  1.47 us

profile of v2, /device:TPU:1, one launch (start us, length us, event | category | flops | bytes accessed | tf_op | source)
XLA Modules:
  0.0 40.1 jit_solution(457687759319841277)
XLA Ops:
  0.6 38.0 %shard_map.77 = (f32[16,16]{1,0:T(8,128)}, f32[4,3600]{1,0:T(4,128)}) custom-call(f32[16,16,3600]{2,1,0:T(8,128)} %patterns.1, bf16[3600,128]{1,0:T(8,128)(2,1)} %bitcast.2, f32[3600]{0:T(1024)} %background.1, s32[16,16]{1,0:T(8,128)} %grain_id.1, s32[16,16]{1,0:T(8,128)} %keep_mask.1, s32[1,32]{1,0:T(1,128)} %bitcast.3), custom_call_target="tpu_custom_call" | custom-call | tf_op jit(solution)/shard_map/pallas_call | solution.py:437
  38.6 1.5 %shard_map.78 = (f32[16,16]{1,0:T(8,128)}, f32[4,3600]{1,0:T(4,128)}) custom-call(f32[16,16]{1,0:T(8,128)} %get-tuple-element.4.found, f32[4,3600]{1,0:T(4,128)} %get-tuple-element.5.sums), custom_call_target="tpu_custom_call" | custom-call | tf_op jit(solution)/shard_map/pallas_call | solution.py:489

commit v3 on v2

--- a/solution.py
+++ b/solution.py
@@ -35,8 +35,8 @@
     D, S, G, TR, TC, pix, R,
     patterns, templates, background, grain_id, keep_mask, grain_row,
     score_out, grain_out,
-    pat, raw, ground, filt, near_mat, pick_mat, halo_mat, sel_mat,
-    edge, corner_src, corner_dst, halo, neigh, indexed, panel,
+    pat, raw, ground, filt, near_mat, halo_mat, sel_mat,
+    edge_rows, edge, corner_src, corner_dst, halo, neigh, indexed, panel,
     gsum, grecv, zbuf, best,
     pat_sem, raw_sem, ground_sem, zsend, nsend, trecv, hsend, hrecv,
     gsend, grecv_sem, zgsend, zgrecv,
@@ -94,16 +94,6 @@
     near_mat[...] = jnp.where(
         near(p0 >> bits, q1 >> bits) & near(p0 & low, q1 & low), 1.0, 0.0
     ).astype(BF16)
-    i0, q = iota((48, points), 0), iota((48, points), 1)
-    k0 = (i0 - 32) >> 1
-    corner_at = jnp.where(
-        k0 == 0, 0, jnp.where(k0 == 1, TC - 1, jnp.where(k0 == 2, points - TC, points - 1))
-    )
-    want = jnp.where(
-        i0 < 16, i0 * TC, jnp.where(i0 < 32, (i0 - 16) * TC + TC - 1,
-                                    jnp.where(i0 < 40, corner_at, -1))
-    )
-    pick_mat[...] = jnp.where(q == want, 1.0, 0.0).astype(BF16)
     p, h = iota((points, 128), 0), iota((points, 128), 1)
     slot, i = h >> 4, h & 15
     r, c = p >> bits, p & low
@@ -149,8 +139,14 @@
     def shard_copy(d, q, ssem, zz, ss):
         return remote(panel.at[d, q], panel.at[d, q], ssem, trecv.at[d, q], zz, ss)
 
-    def z_copy(d, sem_at, zz):
-        return shard_copy(d, piece, zsend.at[sem_at], zz, s)
+    def z_copy(zz):
+        return shard_copy(z, piece, zsend.at[zz], zz, s)
+
+    def z_each(k, act):
+        for step in (k, -k):
+            @pl.when((z + step >= 0) & (z + step < D))
+            def _():
+                act(z_copy(z + step))
 
     def normalise():
         mean = jnp.sum(raw[...].astype(F32), axis=0, keepdims=True) * (1.0 / pix)
@@ -171,10 +167,6 @@
         lower = jnp.where(paired, e % 2 == 1, z > near_end)
         return jnp.where(lower, z - k, z + k)
 
-    def relay(d):
-        target = jnp.where(d < z, z + 1, z - 1)
-        return (target >= 0) & (target < D), target
-
     def piece_sends(d):
         return [
             (piece, 0, first), (piece, 1, second), (piece, 2, piece + twin),
@@ -192,12 +184,6 @@
     def stage_a(e):
         d = event_shard(e)
         arrived(d, piece)
-        on, target = relay(d)
-
-        @pl.when(on)
-        def _():
-            z_copy(d, d, target).start()
-
         for which in (0, 1, 2):
             in_plane(d, which).start()
 
@@ -228,12 +214,6 @@
 
     def stage_end(e):
         d = event_shard(e)
-        on, target = relay(d)
-
-        @pl.when(on)
-        def _():
-            z_copy(d, d, target).wait_send()
-
         for which in range(7):
             in_plane(d, which).wait_send()
 
@@ -265,38 +245,32 @@
     pl.semaphore_wait(barrier, S - 1 + D - 1 + diag_count)
 
 
-    @pl.when(z < D - 1)
-    def _():
-        z_copy(z, z, z + 1).start()
-
-    @pl.when(z > 0)
-    def _():
-        z_copy(z, D, z - 1).start()
+    z_each(1, lambda copy: copy.start())
 
     def filter_rows(a, b):
         for i in range(a, b):
             pat_copy(i).wait()
         centre = centred(pat[a:b] - ground[...].reshape(1, 1, pix), pix)
-        filt[a:b] = unit(centre, pix).astype(BF16)
+        values = unit(centre, pix)
+        filt[a:b] = values.astype(BF16)
+        for i in range(a, b):
+            edge_rows[0, i : i + 1, :] = values[i - a, 0:1, :]
+            edge_rows[1, i : i + 1, :] = values[i - a, TC - 1 : TC, :]
 
     ground_copy.wait()
     filter_rows(TR - 1, TR)
+    filter_rows(0, 1)
     halo_send(0)
-    filter_rows(0, 1)
     halo_send(1)
     for a in range(1, TR - 1, 7):
         filter_rows(a, min(a + 7, TR - 1))
-
-    for a, b in cuts:
-        got = jnp.dot(
-            pick_mat[...], filt[:, :, a:b].reshape(points, b - a), preferred_element_type=F32
-        ).astype(BF16)
-        edge[0, :, a:b] = got[0:16]
-        edge[1, :, a:b] = got[16:32]
-        for k in range(4):
-            corner_src[k, :, a:b] = got[32 + 2 * k : 34 + 2 * k]
+    edge[...] = edge_rows[...].astype(BF16)
+    for k, (side, i) in enumerate([(0, 0), (1, 0), (0, TR - 1), (1, TR - 1)]):
+        corner_src[k] = jnp.broadcast_to(edge_rows[side, i : i + 1, :], (2, pix)).astype(BF16)
     for k in range(2, 8):
         halo_send(k)
+    for k in range(2, D):
+        z_each(k, lambda copy: copy.start())
 
     events = min(D - 1, 3)
     stage_a(1)
@@ -396,13 +370,8 @@
     for k in range(TR):
         score_out[k : k + 1, :] = score_row[:, k * TC : (k + 1) * TC]
 
-    @pl.when(z < D - 1)
-    def _():
-        z_copy(z, z, z + 1).wait_send()
-
-    @pl.when(z > 0)
-    def _():
-        z_copy(z, D, z - 1).wait_send()
+    for k in range(1, D):
+        z_each(k, lambda copy: copy.wait_send())
 
     @pl.loop(1, D)
     def _(e):
@@ -448,9 +417,9 @@
             pltpu.VMEM((1, pix), F32),
             pltpu.VMEM((TR, TC, pix), BF16),
             pltpu.VMEM((points, points), BF16),
-            pltpu.VMEM((48, points), BF16),
             pltpu.VMEM((points, 128), BF16),
             pltpu.VMEM((G, points), BF16),
+            pltpu.VMEM((2, 16, pix), F32),
             pltpu.VMEM((2, 16, pix), BF16),
             pltpu.VMEM((4, 2, pix), BF16),
             pltpu.VMEM((4, 2, pix), BF16),
@@ -465,7 +434,7 @@
             dma((TR,)),
             dma,
             dma,
-            dma((D + 1,)),
+            dma((D,)),
             dma((D, 7)),
             dma((D, GROUP)),
             dma((8,)),

time: 40.3 us -> 43.2 us (1.072)
  Pallas kernels: 39.5 us -> 42.3 us
    pallas_call x1, Pallas kernels: 38 us -> 40.8 us  [shards(): pl.pallas_call(functools.partial(kernel, D, S, G, TR, TC, pix, R), out_sh...]
where the time goes in v3:
time: 43.2 us; the launch traced here: 42.9 us
  Pallas kernels  42.3 us (98%)
  between operations  0.64 us (1%)
    pallas_call x1, Pallas kernels, shards(): pl.pallas_call(functools.partial(kernel, D, S, G, TR, TC, pix, R), out_sh...  40.8 us
    pallas_call x1, Pallas kernels, shards(): pl.pallas_call(hand_over, out_shape=(jax.ShapeDtypeStruct(found.shape, F3...  1.47 us

profile of v3, /device:TPU:1, one launch (start us, length us, event | category | flops | bytes accessed | tf_op | source)
XLA Modules:
  0.0 42.9 jit_solution(14876971788825957044)
XLA Ops:
  0.6 40.8 %shard_map.77 = (f32[16,16]{1,0:T(8,128)}, f32[4,3600]{1,0:T(4,128)}) custom-call(f32[16,16,3600]{2,1,0:T(8,128)} %patterns.1, bf16[3600,128]{1,0:T(8,128)(2,1)} %bitcast.2, f32[3600]{0:T(1024)} %background.1, s32[16,16]{1,0:T(8,128)} %grain_id.1, s32[16,16]{1,0:T(8,128)} %keep_mask.1, s32[1,32]{1,0:T(1,128)} %bitcast.3), custom_call_target="tpu_custom_call" | custom-call | tf_op jit(solution)/shard_map/pallas_call | solution.py:406
  41.4 1.5 %shard_map.78 = (f32[16,16]{1,0:T(8,128)}, f32[4,3600]{1,0:T(4,128)}) custom-call(f32[16,16]{1,0:T(8,128)} %get-tuple-element.4.found, f32[4,3600]{1,0:T(4,128)} %get-tuple-element.5.sums), custom_call_target="tpu_custom_call" | custom-call | tf_op jit(solution)/shard_map/pallas_call | solution.py:458

commit v4 on v3

--- a/solution.py
+++ b/solution.py
@@ -170,7 +170,7 @@
     def piece_sends(d):
         return [
             (piece, 0, first), (piece, 1, second), (piece, 2, piece + twin),
-            (first, 3, second), (first, 4, piece + twin),
+            (piece, 3, across), (first, 4, piece + twin),
             (second, 5, piece + twin), (across, 6, piece + twin),
         ]
 
@@ -184,21 +184,14 @@
     def stage_a(e):
         d = event_shard(e)
         arrived(d, piece)
-        for which in (0, 1, 2):
+        for which in (0, 1, 3, 2):
             in_plane(d, which).start()
 
     def stage_b(e):
         d = event_shard(e)
-        arrived(d, first)
-        for which in (3, 4):
+        for q, which in ((first, 4), (second, 5), (across, 6)):
+            arrived(d, q)
             in_plane(d, which).start()
-
-    def stage_c(e):
-        d = event_shard(e)
-        arrived(d, second)
-        in_plane(d, 5).start()
-        arrived(d, across)
-        in_plane(d, 6).start()
 
     def score(d):
         dots = jnp.dot(
@@ -245,7 +238,8 @@
     pl.semaphore_wait(barrier, S - 1 + D - 1 + diag_count)
 
 
-    z_each(1, lambda copy: copy.start())
+    for k in range(1, min(D, 3)):
+        z_each(k, lambda copy: copy.start())
 
     def filter_rows(a, b):
         for i in range(a, b):
@@ -269,7 +263,7 @@
         corner_src[k] = jnp.broadcast_to(edge_rows[side, i : i + 1, :], (2, pix)).astype(BF16)
     for k in range(2, 8):
         halo_send(k)
-    for k in range(2, D):
+    for k in range(3, D):
         z_each(k, lambda copy: copy.start())
 
     events = min(D - 1, 3)
@@ -314,7 +308,6 @@
     for k in range(1, S):
         grain_copy(lax.rem(s + k, S)).start()
 
-    stage_c(1)
     if events >= 2:
         stage_b(2)
     if events >= 3:
@@ -339,11 +332,9 @@
     for k in range(1, D):
         z_grain(lax.rem(z + k, D), z).start()
 
-    if events >= 2:
-        stage_c(2)
+    stage_d(1)
     if events >= 3:
         stage_b(3)
-    stage_d(1)
     if events >= 2:
         stage_d(2)
 
@@ -356,14 +347,12 @@
     grain_out[...] = unit(held, pix)
 
     if events >= 3:
-        stage_c(3)
         stage_d(3)
     if D > 4:
         @pl.loop(4, D)
         def _(e):
             stage_a(e)
             stage_b(e)
-            stage_c(e)
             stage_d(e)
 
     score_row = jnp.max(best[...].T, axis=0, keepdims=True) * (1.0 / pix**0.5)

time: 43.2 us -> 41.3 us (0.956)
  the two profiles are of different devices: /device:TPU:1 before, /device:TPU:0 now
where the time goes in v4:
time: 41.3 us; the launch traced here: 41 us
  Pallas kernels  40.4 us (98%)
  between operations  0.64 us (2%)
    pallas_call x1, Pallas kernels, shards(): pl.pallas_call(functools.partial(kernel, D, S, G, TR, TC, pix, R), out_sh...  38.9 us
    pallas_call x1, Pallas kernels, shards(): pl.pallas_call(hand_over, out_shape=(jax.ShapeDtypeStruct(found.shape, F3...  1.47 us

profile of v4, /device:TPU:0, one launch (start us, length us, event | category | flops | bytes accessed | tf_op | source)
XLA Modules:
  0.0 41.0 jit_solution(16994230639327017515)
XLA Ops:
  0.6 38.9 %shard_map.77 = (f32[16,16]{1,0:T(8,128)}, f32[4,3600]{1,0:T(4,128)}) custom-call(f32[16,16,3600]{2,1,0:T(8,128)} %patterns.1, bf16[3600,128]{1,0:T(8,128)(2,1)} %bitcast.2, f32[3600]{0:T(1024)} %background.1, s32[16,16]{1,0:T(8,128)} %grain_id.1, s32[16,16]{1,0:T(8,128)} %keep_mask.1, s32[1,32]{1,0:T(1,128)} %bitcast.3), custom_call_target="tpu_custom_call" | custom-call | tf_op jit(solution)/shard_map/pallas_call | solution.py:395
  39.5 1.5 %shard_map.78 = (f32[16,16]{1,0:T(8,128)}, f32[4,3600]{1,0:T(4,128)}) custom-call(f32[16,16]{1,0:T(8,128)} %get-tuple-element.4.found, f32[4,3600]{1,0:T(4,128)} %get-tuple-element.5.sums), custom_call_target="tpu_custom_call" | custom-call | tf_op jit(solution)/shard_map/pallas_call | solution.py:447

commit v5 on v3

--- a/solution.py
+++ b/solution.py
@@ -119,16 +119,21 @@
     to_row = jnp.where(iota((G, G), 0) == grain_row[...], 1.0, 0.0).astype(BF16)
     sel_mat[...] = jnp.dot(to_row, one_hot, preferred_element_type=F32).astype(BF16)
 
-    piece = lax.rem(s, GROUP)
-    base = s - piece
-    core = lax.rem(piece, 2)
-    xbit = lax.rem(piece // 2, 2)
-    ybit = piece // 4
-    px, py = piece + 2 - 4 * xbit, piece + 4 - 8 * ybit
+    in_group = lax.rem(s, GROUP)
+    base = s - in_group
+    core = lax.rem(in_group, 2)
+    chip = in_group // 2
+    xbit = lax.rem(chip, 2)
+    ybit = chip // 2
+    piece = core * 4 + chip
+    px, py = piece + 1 - 2 * xbit, piece + 2 - 4 * ybit
     first = jnp.where(core == 0, px, py)
     second = jnp.where(core == 0, py, px)
-    twin = 1 - 2 * core
     across = first + second - piece
+    twin = piece + 4 - 8 * core
+
+    def holder(q):
+        return base + lax.rem(q, 4) * 2 + q // 4
 
     def remote(src, dst, ssem, rsem, zz, ss):
         return pltpu.make_async_remote_copy(
@@ -139,14 +144,14 @@
     def shard_copy(d, q, ssem, zz, ss):
         return remote(panel.at[d, q], panel.at[d, q], ssem, trecv.at[d, q], zz, ss)
 
-    def z_copy(zz):
-        return shard_copy(z, piece, zsend.at[zz], zz, s)
-
-    def z_each(k, act):
-        for step in (k, -k):
+    def z_copy(d, k, zz):
+        return shard_copy(d, piece, zsend.at[k], zz, s)
+
+    def z_both(act):
+        for k, step in ((z, 1), (D, -1)):
             @pl.when((z + step >= 0) & (z + step < D))
             def _():
-                act(z_copy(z + step))
+                act(z_copy(z, k, z + step))
 
     def normalise():
         mean = jnp.sum(raw[...].astype(F32), axis=0, keepdims=True) * (1.0 / pix)
@@ -167,38 +172,41 @@
         lower = jnp.where(paired, e % 2 == 1, z > near_end)
         return jnp.where(lower, z - k, z + k)
 
-    def piece_sends(d):
-        return [
-            (piece, 0, first), (piece, 1, second), (piece, 2, piece + twin),
-            (first, 3, second), (first, 4, piece + twin),
-            (second, 5, piece + twin), (across, 6, piece + twin),
-        ]
-
-    def in_plane(d, which):
-        q, k, to = piece_sends(d)[which]
-        return shard_copy(d, q, nsend.at[d, k], z, base + to)
+    def relay(d, act):
+        target = jnp.where(d < z, z + 1, z - 1)
+
+        @pl.when((target >= 0) & (target < D))
+        def _():
+            act(z_copy(d, d, target))
+
+    def in_plane(d, k):
+        q, to = ((piece, first), (piece, second), (first, second))[k]
+        return shard_copy(d, q, nsend.at[d, k], z, holder(to))
+
+    def core_copy(d, core):
+        four = panel.at[d, pl.ds(core * 4, 4)]
+        return remote(four, four, nsend.at[d, 3], trecv.at[d, core * 4], z, holder(twin))
 
     def arrived(d, q):
-        shard_copy(d, q, nsend.at[d, 0], z, base + first).wait_recv()
+        shard_copy(d, q, nsend.at[d, 0], z, holder(first)).wait_recv()
 
     def stage_a(e):
         d = event_shard(e)
         arrived(d, piece)
-        for which in (0, 1, 2):
-            in_plane(d, which).start()
+        relay(d, lambda copy: copy.start())
+        in_plane(d, 0).start()
+        in_plane(d, 1).start()
 
     def stage_b(e):
         d = event_shard(e)
         arrived(d, first)
-        for which in (3, 4):
-            in_plane(d, which).start()
+        in_plane(d, 2).start()
 
     def stage_c(e):
         d = event_shard(e)
         arrived(d, second)
-        in_plane(d, 5).start()
         arrived(d, across)
-        in_plane(d, 6).start()
+        core_copy(d, core).start()
 
     def score(d):
         dots = jnp.dot(
@@ -208,14 +216,15 @@
 
     def stage_d(e):
         d = event_shard(e)
-        for q in (piece, first, second, across):
-            arrived(d, q + twin)
+        core_copy(d, 1 - core).wait_recv()
         score(d)
 
     def stage_end(e):
         d = event_shard(e)
-        for which in range(7):
-            in_plane(d, which).wait_send()
+        relay(d, lambda copy: copy.wait_send())
+        for k in range(3):
+            in_plane(d, k).wait_send()
+        core_copy(d, core).wait_send()
 
     halo_moves = [
         (filt.at[TR - 1], halo.at[0], 1, 0),
@@ -245,7 +254,7 @@
     pl.semaphore_wait(barrier, S - 1 + D - 1 + diag_count)
 
 
-    z_each(1, lambda copy: copy.start())
+    z_both(lambda copy: copy.start())
 
     def filter_rows(a, b):
         for i in range(a, b):
@@ -269,18 +278,29 @@
         corner_src[k] = jnp.broadcast_to(edge_rows[side, i : i + 1, :], (2, pix)).astype(BF16)
     for k in range(2, 8):
         halo_send(k)
-    for k in range(2, D):
-        z_each(k, lambda copy: copy.start())
 
     events = min(D - 1, 3)
     stage_a(1)
+    if events >= 3:
+        @pl.when(near_end > 0)
+        def _():
+            stage_a(2)
 
     for a, b in cuts:
         neigh[:, a:b] = jnp.dot(
             near_mat[...], filt[:, :, a:b].reshape(points, b - a), preferred_element_type=F32
         )
     stage_b(1)
-    if events >= 2:
+    if events >= 3:
+        @pl.when(near_end > 0)
+        def _():
+            stage_b(2)
+            stage_a(3)
+
+        @pl.when(near_end == 0)
+        def _():
+            stage_a(2)
+    elif events >= 2:
         stage_a(2)
 
     for k in range(8):
@@ -315,10 +335,18 @@
         grain_copy(lax.rem(s + k, S)).start()
 
     stage_c(1)
-    if events >= 2:
+    if events >= 3:
+        @pl.when(near_end == 0)
+        def _():
+            stage_b(2)
+            stage_a(3)
+
+        @pl.when(near_end > 0)
+        def _():
+            stage_c(2)
+            stage_b(3)
+    elif events >= 2:
         stage_b(2)
-    if events >= 3:
-        stage_a(3)
     best[...] = jnp.full_like(best, -1e30)
     score(z)
 
@@ -339,13 +367,18 @@
     for k in range(1, D):
         z_grain(lax.rem(z + k, D), z).start()
 
-    if events >= 2:
+    stage_d(1)
+    if events >= 3:
+        @pl.when(near_end == 0)
+        def _():
+            stage_c(2)
+            stage_b(3)
+    elif events >= 2:
         stage_c(2)
-    if events >= 3:
-        stage_b(3)
-    stage_d(1)
     if events >= 2:
         stage_d(2)
+    if events >= 3:
+        stage_c(3)
 
     for k in range(1, D):
         source = lax.rem(z + k, D)
@@ -356,7 +389,6 @@
     grain_out[...] = unit(held, pix)
 
     if events >= 3:
-        stage_c(3)
         stage_d(3)
     if D > 4:
         @pl.loop(4, D)
@@ -370,8 +402,7 @@
     for k in range(TR):
         score_out[k : k + 1, :] = score_row[:, k * TC : (k + 1) * TC]
 
-    for k in range(1, D):
-        z_each(k, lambda copy: copy.wait_send())
+    z_both(lambda copy: copy.wait_send())
 
     @pl.loop(1, D)
     def _(e):
@@ -434,8 +465,8 @@
             dma((TR,)),
             dma,
             dma,
-            dma((D,)),
-            dma((D, 7)),
+            dma((D + 1,)),
+            dma((D, 4)),
             dma((D, GROUP)),
             dma((8,)),
             dma((8,)),

time: 43.2 us -> 37.4 us (0.87)
  Pallas kernels: 42.3 us -> 36.5 us
    pallas_call x1, Pallas kernels: 40.8 us -> 35 us  [shards(): pl.pallas_call(functools.partial(kernel, D, S, G, TR, TC, pix, R), out_sh...]
where the time goes in v5:
time: 37.4 us; the launch traced here: 37.1 us
  Pallas kernels  36.5 us (98%)
  between operations  0.64 us (2%)
    pallas_call x1, Pallas kernels, shards(): pl.pallas_call(functools.partial(kernel, D, S, G, TR, TC, pix, R), out_sh...  35 us
    pallas_call x1, Pallas kernels, shards(): pl.pallas_call(hand_over, out_shape=(jax.ShapeDtypeStruct(found.shape, F3...  1.47 us

profile of v5, /device:TPU:1, one launch (start us, length us, event | category | flops | bytes accessed | tf_op | source)
XLA Modules:
  0.0 37.1 jit_solution(10896911851752542459)
XLA Ops:
  0.6 35.0 %shard_map.77 = (f32[16,16]{1,0:T(8,128)}, f32[4,3600]{1,0:T(4,128)}) custom-call(f32[16,16,3600]{2,1,0:T(8,128)} %patterns.1, bf16[3600,128]{1,0:T(8,128)(2,1)} %bitcast.2, f32[3600]{0:T(1024)} %background.1, s32[16,16]{1,0:T(8,128)} %grain_id.1, s32[16,16]{1,0:T(8,128)} %keep_mask.1, s32[1,32]{1,0:T(1,128)} %bitcast.3), custom_call_target="tpu_custom_call" | custom-call | tf_op jit(solution)/shard_map/pallas_call | solution.py:437
  35.6 1.5 %shard_map.78 = (f32[16,16]{1,0:T(8,128)}, f32[4,3600]{1,0:T(4,128)}) custom-call(f32[16,16]{1,0:T(8,128)} %get-tuple-element.4.found, f32[4,3600]{1,0:T(4,128)} %get-tuple-element.5.sums), custom_call_target="tpu_custom_call" | custom-call | tf_op jit(solution)/shard_map/pallas_call | solution.py:489

commit v6 on v5

--- a/solution.py
+++ b/solution.py
@@ -141,17 +141,23 @@
             device_id={"dict": zz, "scan": ss}, device_id_type=MESH,
         )
 
-    def shard_copy(d, q, ssem, zz, ss):
-        return remote(panel.at[d, q], panel.at[d, q], ssem, trecv.at[d, q], zz, ss)
-
-    def z_copy(d, k, zz):
-        return shard_copy(d, piece, zsend.at[k], zz, s)
+    half = run // 32 * 16
+    halves = ((0, 0, run - half), (1, run - half, half))
+
+    def shard_copy(d, q, part, ssem, zz, ss):
+        h, at, size = part
+        rows = panel.at[d, q, pl.ds(at, size)]
+        return remote(rows, rows, ssem, trecv.at[d, q, h], zz, ss)
+
+    def z_copy(d, k, part, zz):
+        return shard_copy(d, piece, part, zsend.at[k, part[0]], zz, s)
 
     def z_both(act):
-        for k, step in ((z, 1), (D, -1)):
-            @pl.when((z + step >= 0) & (z + step < D))
-            def _():
-                act(z_copy(z, k, z + step))
+        for part in halves:
+            for k, step in ((z, 1), (D, -1)):
+                @pl.when((z + step >= 0) & (z + step < D))
+                def _():
+                    act(z_copy(z, k, part, z + step))
 
     def normalise():
         mean = jnp.sum(raw[...].astype(F32), axis=0, keepdims=True) * (1.0 / pix)
@@ -172,40 +178,43 @@
         lower = jnp.where(paired, e % 2 == 1, z > near_end)
         return jnp.where(lower, z - k, z + k)
 
-    def relay(d, act):
+    def relay(d, part, act):
         target = jnp.where(d < z, z + 1, z - 1)
 
         @pl.when((target >= 0) & (target < D))
         def _():
-            act(z_copy(d, d, target))
-
-    def in_plane(d, k):
+            act(z_copy(d, d, part, target))
+
+    def in_plane(d, k, part):
         q, to = ((piece, first), (piece, second), (first, second))[k]
-        return shard_copy(d, q, nsend.at[d, k], z, holder(to))
+        return shard_copy(d, q, part, nsend.at[d, k, part[0]], z, holder(to))
 
     def core_copy(d, core):
         four = panel.at[d, pl.ds(core * 4, 4)]
-        return remote(four, four, nsend.at[d, 3], trecv.at[d, core * 4], z, holder(twin))
-
-    def arrived(d, q):
-        shard_copy(d, q, nsend.at[d, 0], z, holder(first)).wait_recv()
+        return remote(four, four, nsend.at[d, 3, 0], trecv.at[d, core * 4, 0], z, holder(twin))
+
+    def arrived(d, q, part):
+        shard_copy(d, q, part, nsend.at[d, 0, 0], z, holder(first)).wait_recv()
 
     def stage_a(e):
         d = event_shard(e)
-        arrived(d, piece)
-        relay(d, lambda copy: copy.start())
-        in_plane(d, 0).start()
-        in_plane(d, 1).start()
+        for part in halves:
+            arrived(d, piece, part)
+            relay(d, part, lambda copy: copy.start())
+            in_plane(d, 0, part).start()
+            in_plane(d, 1, part).start()
 
     def stage_b(e):
         d = event_shard(e)
-        arrived(d, first)
-        in_plane(d, 2).start()
+        for part in halves:
+            arrived(d, first, part)
+            in_plane(d, 2, part).start()
 
     def stage_c(e):
         d = event_shard(e)
-        arrived(d, second)
-        arrived(d, across)
+        for part in halves:
+            arrived(d, second, part)
+            arrived(d, across, part)
         core_copy(d, core).start()
 
     def score(d):
@@ -221,9 +230,10 @@
 
     def stage_end(e):
         d = event_shard(e)
-        relay(d, lambda copy: copy.wait_send())
-        for k in range(3):
-            in_plane(d, k).wait_send()
+        for part in halves:
+            relay(d, part, lambda copy: copy.wait_send())
+            for k in range(3):
+                in_plane(d, k, part).wait_send()
         core_copy(d, core).wait_send()
 
     halo_moves = [
@@ -339,7 +349,6 @@
         @pl.when(near_end == 0)
         def _():
             stage_b(2)
-            stage_a(3)
 
         @pl.when(near_end > 0)
         def _():
@@ -349,6 +358,11 @@
         stage_b(2)
     best[...] = jnp.full_like(best, -1e30)
     score(z)
+    stage_d(1)
+    if events >= 3:
+        @pl.when(near_end == 0)
+        def _():
+            stage_a(3)
 
     for k in range(1, S):
         source = lax.rem(s + k, S)
@@ -367,7 +381,6 @@
     for k in range(1, D):
         z_grain(lax.rem(z + k, D), z).start()
 
-    stage_d(1)
     if events >= 3:
         @pl.when(near_end == 0)
         def _():
@@ -465,9 +478,9 @@
             dma((TR,)),
             dma,
             dma,
-            dma((D + 1,)),
-            dma((D, 4)),
-            dma((D, GROUP)),
+            dma((D + 1, 2)),
+            dma((D, 4, 2)),
+            dma((D, GROUP, 2)),
             dma((8,)),
             dma((8,)),
             dma((S,)),

time: 37.4 us -> 36.6 us (0.979)
  Pallas kernels: 36.5 us -> 35.7 us
    pallas_call x1, Pallas kernels: 35 us -> 34.3 us  [shards(): pl.pallas_call(functools.partial(kernel, D, S, G, TR, TC, pix, R), out_sh...]
where the time goes in v6:
time: 36.6 us; the launch traced here: 36.4 us
  Pallas kernels  35.7 us (98%)
  between operations  0.64 us (2%)
    pallas_call x1, Pallas kernels, shards(): pl.pallas_call(functools.partial(kernel, D, S, G, TR, TC, pix, R), out_sh...  34.3 us
    pallas_call x1, Pallas kernels, shards(): pl.pallas_call(hand_over, out_shape=(jax.ShapeDtypeStruct(found.shape, F3...  1.47 us

profile of v6, /device:TPU:1, one launch (start us, length us, event | category | flops | bytes accessed | tf_op | source)
XLA Modules:
  0.0 36.4 jit_solution(12490667402903123916)
XLA Ops:
  0.6 34.3 %shard_map.77 = (f32[16,16]{1,0:T(8,128)}, f32[4,3600]{1,0:T(4,128)}) custom-call(f32[16,16,3600]{2,1,0:T(8,128)} %patterns.1, bf16[3600,128]{1,0:T(8,128)(2,1)} %bitcast.2, f32[3600]{0:T(1024)} %background.1, s32[16,16]{1,0:T(8,128)} %grain_id.1, s32[16,16]{1,0:T(8,128)} %keep_mask.1, s32[1,32]{1,0:T(1,128)} %bitcast.3), custom_call_target="tpu_custom_call" | custom-call | tf_op jit(solution)/shard_map/pallas_call | solution.py:450
  34.9 1.5 %shard_map.78 = (f32[16,16]{1,0:T(8,128)}, f32[4,3600]{1,0:T(4,128)}) custom-call(f32[16,16]{1,0:T(8,128)} %get-tuple-element.4.found, f32[4,3600]{1,0:T(4,128)} %get-tuple-element.5.sums), custom_call_target="tpu_custom_call" | custom-call | tf_op jit(solution)/shard_map/pallas_call | solution.py:502
